TPU v7x, 1024 devices: a whole 8x8x8 slice. The times are simulated.
1024 devices in a mesh: row: 32 (over x_lo, y), col: 32 (over x_hi, z, core).
Axes of the slice: x: 8 (x_hi: 2, x_lo: 4; x = x_hi * 4 + x_lo), y: 8, z: 8, core: 2. Of those that a mesh axis runs over, the one named last changes fastest.
Arguments:
- inputs: bfloat16 [128, 12288], P('col', 'row'), may hold values from -6 to 6
- w_in: bfloat16 [12288, 24576], P('row', 'col'), may hold values from -0.0546875 to 0.0546875
- w_out: bfloat16 [24576, 12288], P('col', 'row'), may hold values from -0.0390625 to 0.0390625
- grad_out: bfloat16 [128, 12288], P('col', 'row'), may hold values from -1.5 to 1.5
Outputs:
- grad_in: bfloat16 [128, 12288], P('col', 'row')
- grad_w_in: bfloat16 [12288, 24576], P('row', 'col')
- grad_w_out: bfloat16 [24576, 12288], P('col', 'row')
All inputs are finite; a program needn't handle non-finite values.
Results may differ from a plain program's by a relative error of at most 0.005.
Values may be sent and summed in bfloat16 or wider, within the bound.
A program may use at most 32 MiB of HBM per device.

v0:
```python
import jax
import jax.numpy as jnp
from jax import lax
from jax.sharding import PartitionSpec as P


def gelu_pair(hidden):
    inner = 0.7978845608 * (hidden + 0.044715 * hidden * hidden * hidden)
    tvalue = jnp.tanh(inner)
    value = 0.5 * hidden * (1.0 + tvalue)
    slope = 0.5 * (1.0 + tvalue) + 0.5 * hidden * (1.0 - tvalue * tvalue) * 0.7978845608 * (
        1.0 + 3.0 * 0.044715 * hidden * hidden
    )
    return (value, slope)


def local(inputs, w_in, w_out, grad_out):
    x_panel, dy_panel = (
        lax.all_gather(inputs, "col", axis=0, tiled=True),
        lax.all_gather(grad_out, "col", axis=0, tiled=True),
    )
    rows = x_panel
    pre = lax.psum_scatter(
        jnp.dot(rows, w_in, preferred_element_type=jnp.float32),
        "row",
        scatter_dimension=0,
        tiled=True,
    )
    value, slope = gelu_pair(pre)
    acts = value.astype(jnp.bfloat16)
    dgate = None
    acts_full = lax.all_gather(acts, "row", axis=0, tiled=True)
    rows = dy_panel
    dgate = lax.psum_scatter(
        lax.dot_general(rows, w_out, (((1,), (1,)), ((), ())), preferred_element_type=jnp.float32),
        "row",
        scatter_dimension=0,
        tiled=True,
    )
    delta = (dgate * slope).astype(jnp.bfloat16)
    delta_full = lax.all_gather(delta, "row", axis=0, tiled=True)
    grad_w_out = lax.dot_general(
        acts_full, dy_panel, (((0,), (0,)), ((), ())), preferred_element_type=jnp.float32
    ).astype(jnp.bfloat16)
    grad_w_in = lax.dot_general(
        x_panel, delta_full, (((0,), (0,)), ((), ())), preferred_element_type=jnp.float32
    ).astype(jnp.bfloat16)
    rows = delta_full
    grad_in = lax.psum_scatter(
        lax.dot_general(rows, w_in, (((1,), (1,)), ((), ())), preferred_element_type=jnp.float32),
        "col",
        scatter_dimension=0,
        tiled=True,
    ).astype(jnp.bfloat16)
    return (grad_in, grad_w_in, grad_w_out)


def solution(mesh):
    return jax.shard_map(
        local,
        mesh=mesh,
        in_specs=(P("col", "row"), P("row", "col"), P("col", "row"), P("col", "row")),
        out_specs=(P("col", "row"), P("row", "col"), P("col", "row")),
        check_vma=False,
    )
```

profile of v0, /device:TPU:16, one launch (start us, length us, event | category | flops | bytes accessed | tf_op | source)
XLA Modules:
  0.0 762.2 jit_solution(6603238413264172095)
XLA Ops:
  7.2 0.0 copy-start
  7.2 0.0 copy-start.1
  7.2 0.0 all-reduce.7.cloned.1.call-start
  7.2 66.9 %all-gather = bf16[32,4,384]{2,1,0:T(4,128)(2,1)S(1)} all-gather(bf16[1,4,384]{2,1,0:T(4,128)(2,1)} %bitcast.20), channel_id=1, replica_groups=mesh['row'=32,'col'=32] {'col'}, dimensions={0}, use_global_device_ids=true | all-gather | bytes 101376 | tf_op jit(solution)/shard_map/all_gather | solution.py:20
  74.2 46.8 %all-gather.1 = bf16[32,4,384]{2,1,0:T(4,128)(2,1)S(1)} all-gather(bf16[1,4,384]{2,1,0:T(4,128)(2,1)} %bitcast.21), channel_id=1, replica_groups=mesh['row'=32,'col'=32] {'col'}, dimensions={0}, use_global_device_ids=true | all-gather | bytes 101376 | tf_op jit(solution)/shard_map/all_gather | solution.py:19
  121.1 0.0 copy-done.1
  121.1 1.1 fusion.10
  122.2 0.0 copy-done
  122.2 1.0 fusion.11
  123.2 0.0 all-reduce.7.cloned.1.call-update
  123.2 1.3 dynamic-slice
  124.5 1.3 dynamic-slice.4
  127.1 302.0 %all-reduce.7.cloned.1.call-done = (f32[128,768]{1,0:T(8,128)}, f32[128,768]{1,0:T(8,128)}) async-done(((f32[128,768]{1,0:T(8,128)}, f32[128,768]{1,0:T(8,128)}), (f32[128,768]{1,0:T(8,128)}, f32[128,768]{1,0:T(8,128)})) %all-reduce.7.cloned.1.call-update) | async-done | bytes 786448
  429.0 0.8 fusion.8
  429.8 75.8 %all-gather.2 = bf16[32,4,768]{2,1,0:T(4,128)(2,1)S(1)} all-gather(bf16[1,4,768]{2,1,0:T(4,128)(2,1)S(1)} %get-tuple-element.12), channel_id=1, replica_groups=mesh['row'=32,'col'=32] {'row'}, dimensions={0}, use_global_device_ids=true | all-gather | bytes 202752 | tf_op jit(solution)/shard_map/all_gather | solution.py:41
  505.6 0.1 reshape.11
  505.7 0.3 fusion
  506.0 0.3 fusion.12
  506.4 1.1 copy.8
  507.4 168.4 %all-reduce.8 = bf16[128,384]{1,0:T(8,128)(2,1)S(1)} all-reduce(f32[128,384]{1,0:T(8,128)S(1)} %fusion.12), channel_id=4, replica_groups=mesh['row'=32,'col'=32] {'col'}, use_global_device_ids=true, to_apply=%region_2.0.clone | all-reduce | flops 49152 | bytes 294912
  675.8 77.7 %all-gather.3 = bf16[32,4,768]{2,1,0:T(4,128)(2,1)S(1)} all-gather(bf16[1,4,768]{2,1,0:T(4,128)(2,1)S(1)} %get-tuple-element.11), channel_id=1, replica_groups=mesh['row'=32,'col'=32] {'row'}, dimensions={0}, use_global_device_ids=true | all-gather | bytes 202752 | tf_op jit(solution)/shard_map/all_gather | solution.py:32
  753.5 0.1 reshape.13
  753.6 1.2 convolution_convert_fusion
  754.8 0.6 dynamic-slice_convert_fusion
  (2 shorter events, 0.1 us)
Async XLA Ops:
  7.2 115.0 %copy-start = (bf16[384,768]{1,0:T(8,128)(2,1)S(1)}, bf16[384,768]{1,0:T(8,128)(2,1)}, u32[]{:S(2)}) copy-start(bf16[384,768]{1,0:T(8,128)(2,1)} %param.5) | copy-start | bytes 1769476
  7.2 113.9 %copy-start.1 = (bf16[768,384]{1,0:T(8,128)(2,1)S(1)}, bf16[768,384]{1,0:T(8,128)(2,1)}, u32[]{:S(2)}) copy-start(bf16[768,384]{1,0:T(8,128)(2,1)} %param.6) | copy-start | bytes 1769476
  7.2 421.9 %all-reduce.7.cloned.1.call-start = ((), (), s32[]{:S(2)}) async-start(), calls=%async_computation | async-start | bytes 1572864
Sparse Core Ops, SparseCore 0:
  123.3 305.6 all-reduce.6
where the time goes:
time: 762 us
  blocking collectives  436 us (57%)
  waiting for transfers between devices  302 us (40%)
  between operations  15.4 us (2%)
    unnamed x2, waiting for transfers between devices  302 us
    unnamed x1, blocking collectives  168 us
    all_gather x1, blocking collectives, local(): acts_full = lax.all_gather(acts, 'row', axis=0, tiled=True)  77.7 us
    all_gather x1, blocking collectives, local(): delta_full = lax.all_gather(delta, 'row', axis=0, tiled=True)  75.8 us
    all_gather x1, blocking collectives, local(): lax.all_gather(grad_out, 'col', axis=0, tiled=True)  66.9 us
    all_gather x1, blocking collectives, local(): lax.all_gather(inputs, 'col', axis=0, tiled=True)  46.8 us
  transfers between devices with their start and end apart: 1, of which 1 were waited for; matrix products, arithmetic and copies ran while one was open for 0% of the time, Pallas kernels for 0%

commit v1 on v0

v1 whole, which is shorter than its diff:
```python
import itertools

import jax
import jax.numpy as jnp
from jax import lax
from jax.experimental import pallas as pl
from jax.experimental.pallas import tpu as pltpu
from jax.sharding import PartitionSpec as P

MESH = pl.DeviceIdType.MESH
BF16, F32 = jnp.bfloat16, jnp.float32
SIZES = dict(x_lo=4, y=8, x_hi=2, z=8, core=2)
ROWS, COLS = 32, 32
SLAB = 4
TOKENS = 128
WIDTH, HIDDEN = 384, 768
HALF = HIDDEN // 2
GROUPS = TOKENS // 8


def coordinates():
    row, col = lax.axis_index("row"), lax.axis_index("col")
    return dict(x_lo=row // 8, y=row % 8, x_hi=col // 16, z=(col // 2) % 8, core=col % 2)


def moved(me, **offsets):
    at = dict(me)
    for axis, offset in offsets.items():
        at[axis] = lax.rem(me[axis] + offset, SIZES[axis])
    return at


def device(at):
    return (at["x_lo"] * 8 + at["y"], at["x_hi"] * 16 + at["z"] * 2 + at["core"])


def shard_of(at):
    return at["x_lo"] * 8 + at["y"]


def gelu_value(hidden, tvalue):
    return 0.5 * hidden * (1.0 + tvalue)


def gelu_slope(hidden, tvalue):
    return 0.5 * (1.0 + tvalue) + 0.5 * hidden * (1.0 - tvalue * tvalue) * 0.7978845608 * (
        1.0 + 3.0 * 0.044715 * hidden * hidden
    )


def send(src, dst, send_sem, recv_sem, to):
    pltpu.make_async_remote_copy(
        src_ref=src, dst_ref=dst, send_sem=send_sem, recv_sem=recv_sem,
        device_id=to, device_id_type=MESH,
    ).start()


def drain(ref, sem):
    pltpu.make_async_copy(ref, ref, sem).wait()


def kernel(
    x_hbm, w_in_hbm, w_out_hbm, dy_hbm,
    gi_ref, gwi_ref, gwo_ref,
    x_raw, dy_raw, w_in, w_out, panels, part_out, part_in, hidden_grads, pair_out, pair_in, gi_out, gi_in,
    local_sems, send_sems, recv_sems,
):
    me = coordinates()
    shard, core, z = shard_of(me), me["core"], me["z"]
    sibling = moved(me, core=1)
    near = [moved(me, z=j) for j in (4, 3, 5, 2, 6, 1, 7)]
    far = [moved(me, x_hi=1, z=j) for j in (4, 3, 5, 2, 6, 1, 7, 0)]
    row_peers = [
        moved(me, x_lo=i, y=j)
        for i, j in sorted(itertools.product(range(4), range(8)), key=lambda o: -min(o[1], 8 - o[1]) - o[0])
        if (i, j) != (0, 0)
    ]
    upper = lax.broadcasted_iota(jnp.int32, (1, 8, 1), 1) < SLAB
    upper_rows = lax.broadcasted_iota(jnp.int32, (TOKENS, 1), 0) % 8 < SLAB
    pending = []

    loads = [
        pltpu.make_async_copy(x_hbm, x_raw, local_sems.at[0]),
        pltpu.make_async_copy(dy_hbm, dy_raw, local_sems.at[1]),
        pltpu.make_async_copy(w_in_hbm, w_in, local_sems.at[2]),
        pltpu.make_async_copy(w_out_hbm, w_out, local_sems.at[3]),
    ]
    for load in loads:
        load.start()

    barrier = pltpu.get_barrier_semaphore()
    for to in [*far, *near, *row_peers, sibling]:
        pl.semaphore_signal(barrier, inc=1, device_id=device(to), device_id_type=MESH)
    loads[0].wait()
    loads[1].wait()
    panels[0, core, z] = jnp.concatenate([x_raw[...].astype(F32), dy_raw[...].astype(F32)], axis=0).astype(BF16)
    pl.semaphore_wait(barrier, len(far) + len(near) + len(row_peers) + 1)

    own = panels.at[0, core, z]
    for to in far:
        send(own, panels.at[1, core, z], send_sems.at[10], recv_sems.at[1], device(to))
    for to in near:
        send(own, own, send_sems.at[0], recv_sems.at[0], device(to))
    pending.append((panels.at[1, 0], send_sems.at[10]))
    pending.append((panels.at[0, 0, pl.ds(0, 7)], send_sems.at[0]))

    def partial_sums(chunk):
        rows = panels.at[chunk, core]
        drain(rows if chunk else panels.at[0, core, pl.ds(0, 7)], recv_sems.at[chunk])
        send(rows, rows, send_sems.at[1 + chunk], recv_sems.at[2 + chunk], device(sibling))
        pending.append((rows, send_sems.at[1 + chunk]))
        drain(rows, recv_sems.at[2 + chunk])
        if chunk == 0:
            loads[2].wait()
            loads[3].wait()
        stacked = panels[chunk].reshape(TOKENS, WIDTH)
        pre = jnp.dot(stacked, w_in[...], preferred_element_type=F32)
        dgate = lax.dot_general(stacked, w_out[...], (((1,), (1,)), ((), ())), preferred_element_type=F32)
        both = jnp.where(upper_rows, pre, dgate)
        for h in range(2):
            part_out[chunk, pl.ds(h * GROUPS, GROUPS)] = (
                both[:, h * HALF : (h + 1) * HALF].reshape(GROUPS, 8, HALF).astype(BF16)
            )
        for to in row_peers:
            send(
                part_out.at[chunk, shard_of(to)], part_in.at[chunk, shard],
                send_sems.at[3 + chunk], recv_sems.at[4 + chunk], device(to),
            )
        part_in[chunk, shard] = part_out[chunk, shard]
        pending.append((part_in.at[chunk, pl.ds(0, 31)], send_sems.at[3 + chunk]))

    def activate(chunk):
        drain(part_in.at[chunk, pl.ds(0, 31)], recv_sems.at[4 + chunk])
        total = jnp.sum(part_in[chunk].astype(F32), axis=0)
        tvalue = jnp.tanh(0.7978845608 * (total + 0.044715 * total * total * total))
        slope = pltpu.roll(gelu_slope(total, tvalue), SLAB, 0)
        hidden_grads[chunk, shard] = jnp.where(upper[0], gelu_value(total, tvalue), total * slope).astype(BF16)
        for to in row_peers:
            mine = hidden_grads.at[chunk, shard]
            send(mine, mine, send_sems.at[5 + chunk], recv_sems.at[6 + chunk], device(to))
        pending.append((hidden_grads.at[chunk, pl.ds(0, 31)], send_sems.at[5 + chunk]))

    def half_of(chunk, h):
        return hidden_grads[chunk, pl.ds(h * GROUPS, GROUPS)].reshape(TOKENS, HALF)

    def input_grads(chunk):
        drain(hidden_grads.at[chunk, pl.ds(0, 31)], recv_sems.at[6 + chunk])
        gi = sum(
            lax.dot_general(
                half_of(chunk, h), w_in[:, h * HALF : (h + 1) * HALF],
                (((1,), (1,)), ((), ())), preferred_element_type=F32,
            )
            for h in range(2)
        ).reshape(2, 8, 8, WIDTH)
        ours = jnp.where(core == 0, gi[0], gi[1])
        pair_out[chunk] = jnp.where(core == 0, gi[1], gi[0])
        send(pair_out.at[chunk], pair_in.at[chunk], send_sems.at[7 + chunk], recv_sems.at[8 + chunk], device(sibling))
        pending.append((pair_in.at[chunk], send_sems.at[7 + chunk]))
        drain(pair_in.at[chunk], recv_sems.at[8 + chunk])
        ours = ours + pair_in[chunk]
        high = ours.astype(BF16).astype(F32)
        low = pltpu.roll(ours - high, SLAB, 1)
        gi_out[chunk] = jnp.where(upper, low, high).astype(BF16)
        for to in far if chunk else near:
            send(
                gi_out.at[chunk, to["z"]], gi_in.at[chunk, z],
                send_sems.at[11 if chunk else 9], recv_sems.at[10 + chunk], device(to),
            )
        if chunk == 0:
            gi_in[0, z] = gi_out[0, z]

    partial_sums(0)
    partial_sums(1)
    activate(0)
    activate(1)
    input_grads(0)
    input_grads(1)

    wide = panels[...].astype(F32).reshape(2, GROUPS, 8, WIDTH)
    swapped = pltpu.roll(wide.reshape(2 * GROUPS, 8, WIDTH), SLAB, 1)
    grads_out = swapped.reshape(2 * TOKENS, WIDTH).astype(BF16)
    only_inputs = jnp.where(upper, 0.0, swapped).reshape(2 * TOKENS, WIDTH).astype(BF16)
    for h in range(2):
        both = jnp.concatenate([half_of(chunk, h) for chunk in range(2)], axis=0)
        only_acts = jnp.where(upper, both.astype(F32).reshape(2 * GROUPS, 8, HALF), 0.0)
        gwo_ref[pl.ds(h * HALF, HALF), :] = lax.dot_general(
            only_acts.reshape(2 * TOKENS, HALF).astype(BF16), grads_out,
            (((0,), (0,)), ((), ())), preferred_element_type=F32,
        ).astype(BF16)
        gwi_ref[:, pl.ds(h * HALF, HALF)] = lax.dot_general(
            only_inputs, both, (((0,), (0,)), ((), ())), preferred_element_type=F32
        ).astype(BF16)

    drain(gi_in.at[0, pl.ds(0, 7)], recv_sems.at[10])
    drain(gi_in.at[1], recv_sems.at[11])
    total = jnp.sum(gi_in[...].astype(F32).reshape(16, 8, WIDTH), axis=0)
    gi_ref[...] = (total[:SLAB] + total[SLAB:]).astype(BF16)

    pending.append((gi_in.at[0, pl.ds(0, 7)], send_sems.at[9]))
    pending.append((gi_in.at[1], send_sems.at[11]))
    for copy in pending:
        drain(*copy)


def write_out(gi, gwi, gwo, gi_hbm, gwi_hbm, gwo_hbm, sems):
    copies = [
        pltpu.make_async_copy(gi, gi_hbm, sems.at[0]),
        pltpu.make_async_copy(gwi, gwi_hbm, sems.at[1]),
        pltpu.make_async_copy(gwo, gwo_hbm, sems.at[2]),
    ]
    for copy in copies:
        copy.start()
    for copy in copies:
        copy.wait()


def local(inputs, w_in, w_out, grad_out):
    hbm = pl.BlockSpec(memory_space=pltpu.HBM)
    vmem = pl.BlockSpec(memory_space=pltpu.VMEM)
    outs = pl.pallas_call(
        kernel,
        out_shape=(
            jax.ShapeDtypeStruct((SLAB, WIDTH), BF16),
            jax.ShapeDtypeStruct((WIDTH, HIDDEN), BF16),
            jax.ShapeDtypeStruct((HIDDEN, WIDTH), BF16),
        ),
        in_specs=[hbm] * 4,
        out_specs=(vmem, vmem, vmem),
        scratch_shapes=[
            pltpu.VMEM((SLAB, WIDTH), BF16),
            pltpu.VMEM((SLAB, WIDTH), BF16),
            pltpu.VMEM((WIDTH, HIDDEN), BF16),
            pltpu.VMEM((HIDDEN, WIDTH), BF16),
            pltpu.VMEM((2, 2, 8, 8, WIDTH), BF16),
            pltpu.VMEM((2, ROWS, 8, HALF), BF16),
            pltpu.VMEM((2, ROWS, 8, HALF), BF16),
            pltpu.VMEM((2, ROWS, 8, HALF), BF16),
            pltpu.VMEM((2, 8, 8, WIDTH), F32),
            pltpu.VMEM((2, 8, 8, WIDTH), F32),
            pltpu.VMEM((2, 8, 8, WIDTH), BF16),
            pltpu.VMEM((2, 8, 8, WIDTH), BF16),
            pltpu.SemaphoreType.DMA((4,)),
            pltpu.SemaphoreType.DMA((12,)),
            pltpu.SemaphoreType.DMA((12,)),
        ],
        compiler_params=pltpu.CompilerParams(
            collective_id=0, has_side_effects=True, vmem_limit_bytes=62 * 2**20
        ),
        name="ffn_backward",
    )(inputs, w_in, w_out, grad_out)
    return pl.pallas_call(
        write_out,
        out_shape=tuple(jax.ShapeDtypeStruct(out.shape, out.dtype) for out in outs),
        in_specs=[vmem] * 3,
        out_specs=(hbm, hbm, hbm),
        scratch_shapes=[pltpu.SemaphoreType.DMA((3,))],
        name="write_out",
    )(*outs)


def solution(mesh):
    return jax.shard_map(
        local,
        mesh=mesh,
        in_specs=(P("col", "row"), P("row", "col"), P("col", "row"), P("col", "row")),
        out_specs=(P("col", "row"), P("row", "col"), P("col", "row")),
        check_vma=False,
    )
```

time: 762 us -> 64.5 us (0.08)
  the two profiles are of different devices: /device:TPU:16 before, /device:TPU:15 now
where the time goes in v1:
time: 64.5 us; the launch traced here: 63.7 us
  Pallas kernels  63 us (98%)
    pallas_call x1, Pallas kernels, local(): pl.pallas_call(kernel, out_shape=(jax.ShapeDtypeStruct((SLAB, WIDTH), BF1...  60.7 us
    pallas_call x1, Pallas kernels, local(): pl.pallas_call(write_out, out_shape=tuple((jax.ShapeDtypeStruct(out.shape...  2.29 us

profile of v1, /device:TPU:15, one launch (start us, length us, event | category | flops | bytes accessed | tf_op | source)
XLA Modules:
  0.0 63.7 jit_solution(266283196997010412)
XLA Ops:
  0.6 60.7 %ffn_backward.1 = (bf16[4,384]{1,0:T(4,128)(2,1)}, bf16[384,768]{1,0:T(8,128)(2,1)}, bf16[768,384]{1,0:T(8,128)(2,1)}) custom-call(bf16[4,384]{1,0:T(4,128)(2,1)} %x_hbm.1, bf16[384,768]{1,0:T(8,128)(2,1)} %w_in_hbm.1, bf16[768,384]{1,0:T(8,128)(2,1)} %w_out_hbm.1, bf16[4,384]{1,0:T(4,128)(2,1)} %dy_hbm.1), custom_call_target="tpu_custom_call" | custom-call | tf_op jit(solution)/shard_map/ffn_backward/pallas_call | solution.py:220
  61.4 2.3 %write_out.1 = (bf16[4,384]{1,0:T(4,128)(2,1)}, bf16[384,768]{1,0:T(8,128)(2,1)}, bf16[768,384]{1,0:T(8,128)(2,1)}) custom-call(bf16[4,384]{1,0:T(4,128)(2,1)} %get-tuple-element.6.gi, bf16[384,768]{1,0:T(8,128)(2,1)} %get-tuple-element.7.gwi, bf16[768,384]{1,0:T(8,128)(2,1)} %get-tuple-element.8.gwo), custom_call_target="tpu_custom_call" | custom-call | tf_op jit(solution)/shard_map/write_out/pallas_call | solution.py:251

commit v2 on v1

--- a/solution.py
+++ b/solution.py
@@ -16,6 +16,7 @@
 WIDTH, HIDDEN = 384, 768
 HALF = HIDDEN // 2
 GROUPS = TOKENS // 8
+PIECES = 4
 
 
 def coordinates():
@@ -61,9 +62,9 @@
 
 def kernel(
     x_hbm, w_in_hbm, w_out_hbm, dy_hbm,
-    gi_ref, gwi_ref, gwo_ref,
-    x_raw, dy_raw, w_in, w_out, panels, part_out, part_in, hidden_grads, pair_out, pair_in, gi_out, gi_in,
-    local_sems, send_sems, recv_sems,
+    gi_ref, gwi_hbm, gwo_hbm,
+    gwi_ref, gwo_ref, x_raw, dy_raw, w_in, w_out, panels, part_out, part_in, hidden_grads, gi_out, gi_in,
+    local_sems, send_sems, recv_sems, relay,
 ):
     me = coordinates()
     shard, core, z = shard_of(me), me["core"], me["z"]
@@ -88,19 +89,23 @@
     for load in loads:
         load.start()
 
+    lines = [moved(me, y=j) for j in (4, 3, 5, 2, 6, 1, 7)]
+    greeted = [*far, *near, *lines, *[moved(me, x_lo=i) for i in (3, 2, 1)], sibling]
     barrier = pltpu.get_barrier_semaphore()
-    for to in [*far, *near, *row_peers, sibling]:
+    for to in greeted:
         pl.semaphore_signal(barrier, inc=1, device_id=device(to), device_id_type=MESH)
     loads[0].wait()
     loads[1].wait()
     panels[0, core, z] = jnp.concatenate([x_raw[...].astype(F32), dy_raw[...].astype(F32)], axis=0).astype(BF16)
-    pl.semaphore_wait(barrier, len(far) + len(near) + len(row_peers) + 1)
+    pl.semaphore_wait(barrier, len(greeted))
 
     own = panels.at[0, core, z]
     for to in far:
         send(own, panels.at[1, core, z], send_sems.at[10], recv_sems.at[1], device(to))
     for to in near:
         send(own, own, send_sems.at[0], recv_sems.at[0], device(to))
+    for to in lines:
+        pl.semaphore_signal(relay, inc=1, device_id=device(to), device_id_type=MESH)
     pending.append((panels.at[1, 0], send_sems.at[10]))
     pending.append((panels.at[0, 0, pl.ds(0, 7)], send_sems.at[0]))
 
@@ -113,6 +118,7 @@
         if chunk == 0:
             loads[2].wait()
             loads[3].wait()
+            pl.semaphore_wait(relay, len(lines))
         stacked = panels[chunk].reshape(TOKENS, WIDTH)
         pre = jnp.dot(stacked, w_in[...], preferred_element_type=F32)
         dgate = lax.dot_general(stacked, w_out[...], (((1,), (1,)), ((), ())), preferred_element_type=F32)
@@ -151,23 +157,17 @@
                 (((1,), (1,)), ((), ())), preferred_element_type=F32,
             )
             for h in range(2)
-        ).reshape(2, 8, 8, WIDTH)
-        ours = jnp.where(core == 0, gi[0], gi[1])
-        pair_out[chunk] = jnp.where(core == 0, gi[1], gi[0])
-        send(pair_out.at[chunk], pair_in.at[chunk], send_sems.at[7 + chunk], recv_sems.at[8 + chunk], device(sibling))
-        pending.append((pair_in.at[chunk], send_sems.at[7 + chunk]))
-        drain(pair_in.at[chunk], recv_sems.at[8 + chunk])
-        ours = ours + pair_in[chunk]
-        high = ours.astype(BF16).astype(F32)
-        low = pltpu.roll(ours - high, SLAB, 1)
-        gi_out[chunk] = jnp.where(upper, low, high).astype(BF16)
-        for to in far if chunk else near:
+        ).reshape(GROUPS, 8, WIDTH)
+        gi_out[chunk] = gi[:, SLAB:].astype(BF16)
+        there = far if chunk else near
+        both = [*there, *[moved(to, core=1) for to in there], *([] if chunk else [sibling])]
+        for to in both:
             send(
-                gi_out.at[chunk, to["z"]], gi_in.at[chunk, z],
-                send_sems.at[11 if chunk else 9], recv_sems.at[10 + chunk], device(to),
+                gi_out.at[chunk, to["core"] * 8 + to["z"]], gi_in.at[chunk, core * 8 + z],
+                send_sems.at[7 + chunk], recv_sems.at[8 + chunk], device(to),
             )
         if chunk == 0:
-            gi_in[0, z] = gi_out[0, z]
+            gi_in[0, core * 8 + z] = gi_out[0, core * 8 + z]
 
     partial_sums(0)
     partial_sums(1)
@@ -191,27 +191,45 @@
             only_inputs, both, (((0,), (0,)), ((), ())), preferred_element_type=F32
         ).astype(BF16)
 
-    drain(gi_in.at[0, pl.ds(0, 7)], recv_sems.at[10])
-    drain(gi_in.at[1], recv_sems.at[11])
-    total = jnp.sum(gi_in[...].astype(F32).reshape(16, 8, WIDTH), axis=0)
-    gi_ref[...] = (total[:SLAB] + total[SLAB:]).astype(BF16)
-
-    pending.append((gi_in.at[0, pl.ds(0, 7)], send_sems.at[9]))
-    pending.append((gi_in.at[1], send_sems.at[11]))
+    stores = [
+        pltpu.make_async_copy(gwi_ref, gwi_hbm, local_sems.at[4]),
+        pltpu.make_async_copy(gwo_ref, gwo_hbm, local_sems.at[5]),
+    ]
+    for store in stores:
+        store.start()
+    nearby, distant = gi_in.at[0, pl.ds(0, 15)], gi_in.at[1]
+    drain(nearby, recv_sems.at[8])
+    drain(distant, recv_sems.at[9])
+    gi_ref[...] = jnp.sum(gi_in[...].astype(F32).reshape(32, SLAB, WIDTH), axis=0).astype(BF16)
+
+    pending.append((nearby, send_sems.at[7]))
+    pending.append((distant, send_sems.at[8]))
+    for store in stores:
+        store.wait()
     for copy in pending:
         drain(*copy)
 
 
-def write_out(gi, gwi, gwo, gi_hbm, gwi_hbm, gwo_hbm, sems):
-    copies = [
-        pltpu.make_async_copy(gi, gi_hbm, sems.at[0]),
-        pltpu.make_async_copy(gwi, gwi_hbm, sems.at[1]),
-        pltpu.make_async_copy(gwo, gwo_hbm, sems.at[2]),
-    ]
-    for copy in copies:
-        copy.start()
-    for copy in copies:
-        copy.wait()
+def write_out(gi, gwi, gwo, gi_hbm, gwi_hbm, gwo_hbm, gi_vmem, gwi_vmem, gwo_vmem, in_sems, out_sems):
+    loads, stores = [], []
+
+    def through(source, held, target, pieces):
+        rows = source.shape[0] // pieces
+        for piece in range(pieces):
+            part, at = pl.ds(piece * rows, rows), len(loads)
+            loads.append(pltpu.make_async_copy(source.at[part], held.at[part], in_sems.at[at]))
+            stores.append(pltpu.make_async_copy(held.at[part], target.at[part], out_sems.at[at]))
+
+    through(gwi, gwi_vmem, gwi_hbm, PIECES)
+    through(gwo, gwo_vmem, gwo_hbm, PIECES)
+    through(gi, gi_vmem, gi_hbm, 1)
+    for load in loads:
+        load.start()
+    for load, store in zip(loads, stores):
+        load.wait()
+        store.start()
+    for store in stores:
+        store.wait()
 
 
 def local(inputs, w_in, w_out, grad_out):
@@ -225,8 +243,10 @@
             jax.ShapeDtypeStruct((HIDDEN, WIDTH), BF16),
         ),
         in_specs=[hbm] * 4,
-        out_specs=(vmem, vmem, vmem),
+        out_specs=(vmem, hbm, hbm),
         scratch_shapes=[
+            pltpu.VMEM((WIDTH, HIDDEN), BF16),
+            pltpu.VMEM((HIDDEN, WIDTH), BF16),
             pltpu.VMEM((SLAB, WIDTH), BF16),
             pltpu.VMEM((SLAB, WIDTH), BF16),
             pltpu.VMEM((WIDTH, HIDDEN), BF16),
@@ -235,13 +255,12 @@
             pltpu.VMEM((2, ROWS, 8, HALF), BF16),
             pltpu.VMEM((2, ROWS, 8, HALF), BF16),
             pltpu.VMEM((2, ROWS, 8, HALF), BF16),
-            pltpu.VMEM((2, 8, 8, WIDTH), F32),
-            pltpu.VMEM((2, 8, 8, WIDTH), F32),
-            pltpu.VMEM((2, 8, 8, WIDTH), BF16),
-            pltpu.VMEM((2, 8, 8, WIDTH), BF16),
-            pltpu.SemaphoreType.DMA((4,)),
+            pltpu.VMEM((2, GROUPS, SLAB, WIDTH), BF16),
+            pltpu.VMEM((2, GROUPS, SLAB, WIDTH), BF16),
+            pltpu.SemaphoreType.DMA((6,)),
             pltpu.SemaphoreType.DMA((12,)),
             pltpu.SemaphoreType.DMA((12,)),
+            pltpu.SemaphoreType.REGULAR,
         ],
         compiler_params=pltpu.CompilerParams(
             collective_id=0, has_side_effects=True, vmem_limit_bytes=62 * 2**20
@@ -251,9 +270,13 @@
     return pl.pallas_call(
         write_out,
         out_shape=tuple(jax.ShapeDtypeStruct(out.shape, out.dtype) for out in outs),
-        in_specs=[vmem] * 3,
+        in_specs=[hbm, hbm, hbm],
         out_specs=(hbm, hbm, hbm),
-        scratch_shapes=[pltpu.SemaphoreType.DMA((3,))],
+        scratch_shapes=[
+            *[pltpu.VMEM(out.shape, out.dtype) for out in outs],
+            pltpu.SemaphoreType.DMA((1 + 2 * PIECES,)),
+            pltpu.SemaphoreType.DMA((1 + 2 * PIECES,)),
+        ],
         name="write_out",
     )(*outs)
 

time: 64.5 us -> 62.9 us (0.975); the launches traced: 63.7 us -> 62.8 us
  Pallas kernels: 63 us -> 62.1 us
    pallas_call x1, Pallas kernels: 60.7 us -> 59.9 us  [local(): pl.pallas_call(kernel, out_shape=(jax.ShapeDtypeStruct((SLAB, WIDTH), BF1...]
where the time goes in v2:
time: 62.9 us; the launch traced here: 62.8 us
  Pallas kernels  62.1 us (99%)
  between operations  0.64 us (1%)
    pallas_call x1, Pallas kernels, local(): pl.pallas_call(kernel, out_shape=(jax.ShapeDtypeStruct((SLAB, WIDTH), BF1...  59.9 us
    pallas_call x1, Pallas kernels, local(): pl.pallas_call(write_out, out_shape=tuple((jax.ShapeDtypeStruct(out.shape...  2.17 us

profile of v2, /device:TPU:15, one launch (start us, length us, event | category | flops | bytes accessed | tf_op | source)
XLA Modules:
  0.0 62.8 jit_solution(7535621600571885073)
XLA Ops:
  0.6 59.9 %ffn_backward.1 = (bf16[4,384]{1,0:T(4,128)(2,1)}, bf16[384,768]{1,0:T(8,128)(2,1)}, bf16[768,384]{1,0:T(8,128)(2,1)}) custom-call(bf16[4,384]{1,0:T(4,128)(2,1)} %x_hbm.1, bf16[384,768]{1,0:T(8,128)(2,1)} %w_in_hbm.1, bf16[768,384]{1,0:T(8,128)(2,1)} %w_out_hbm.1, bf16[4,384]{1,0:T(4,128)(2,1)} %dy_hbm.1), custom_call_target="tpu_custom_call" | custom-call | tf_op jit(solution)/shard_map/ffn_backward/pallas_call | solution.py:238
  60.6 2.2 %write_out.1 = (bf16[4,384]{1,0:T(4,128)(2,1)}, bf16[384,768]{1,0:T(8,128)(2,1)}, bf16[768,384]{1,0:T(8,128)(2,1)}) custom-call(bf16[4,384]{1,0:T(4,128)(2,1)} %get-tuple-element.6.gi, bf16[384,768]{1,0:T(8,128)(2,1)} %get-tuple-element.7.gwi, bf16[768,384]{1,0:T(8,128)(2,1)} %get-tuple-element.8.gwo), custom_call_target="tpu_custom_call" | custom-call | tf_op jit(solution)/shard_map/write_out/pallas_call | solution.py:270

commit v3 on v2

--- a/solution.py
+++ b/solution.py
@@ -62,8 +62,8 @@
 
 def kernel(
     x_hbm, w_in_hbm, w_out_hbm, dy_hbm,
-    gi_ref, gwi_hbm, gwo_hbm,
-    gwi_ref, gwo_ref, x_raw, dy_raw, w_in, w_out, panels, part_out, part_in, hidden_grads, gi_out, gi_in,
+    gi_in, gwi_hbm, gwo_hbm,
+    gwi_ref, gwo_ref, x_raw, dy_raw, w_in, w_out, panels, part_out, part_in, hidden_grads, gi_out,
     local_sems, send_sems, recv_sems, relay,
 ):
     me = coordinates()
@@ -78,7 +78,7 @@
     ]
     upper = lax.broadcasted_iota(jnp.int32, (1, 8, 1), 1) < SLAB
     upper_rows = lax.broadcasted_iota(jnp.int32, (TOKENS, 1), 0) % 8 < SLAB
-    pending = []
+    pending, stores = [], []
 
     loads = [
         pltpu.make_async_copy(x_hbm, x_raw, local_sems.at[0]),
@@ -160,14 +160,17 @@
         ).reshape(GROUPS, 8, WIDTH)
         gi_out[chunk] = gi[:, SLAB:].astype(BF16)
         there = far if chunk else near
-        both = [*there, *[moved(to, core=1) for to in there], *([] if chunk else [sibling])]
+        both = [at for to in there for at in (to, moved(to, core=1))] + ([] if chunk else [sibling])
         for to in both:
             send(
                 gi_out.at[chunk, to["core"] * 8 + to["z"]], gi_in.at[chunk, core * 8 + z],
                 send_sems.at[7 + chunk], recv_sems.at[8 + chunk], device(to),
             )
         if chunk == 0:
-            gi_in[0, core * 8 + z] = gi_out[0, core * 8 + z]
+            stores.append(pltpu.make_async_copy(
+                gi_out.at[0, core * 8 + z], gi_in.at[0, core * 8 + z], local_sems.at[6]
+            ))
+            stores[0].start()
 
     partial_sums(0)
     partial_sums(1)
@@ -191,17 +194,13 @@
             only_inputs, both, (((0,), (0,)), ((), ())), preferred_element_type=F32
         ).astype(BF16)
 
-    stores = [
-        pltpu.make_async_copy(gwi_ref, gwi_hbm, local_sems.at[4]),
-        pltpu.make_async_copy(gwo_ref, gwo_hbm, local_sems.at[5]),
-    ]
-    for store in stores:
-        store.start()
+    stores.append(pltpu.make_async_copy(gwi_ref, gwi_hbm, local_sems.at[4]))
+    stores.append(pltpu.make_async_copy(gwo_ref, gwo_hbm, local_sems.at[5]))
+    stores[1].start()
+    stores[2].start()
     nearby, distant = gi_in.at[0, pl.ds(0, 15)], gi_in.at[1]
     drain(nearby, recv_sems.at[8])
     drain(distant, recv_sems.at[9])
-    gi_ref[...] = jnp.sum(gi_in[...].astype(F32).reshape(32, SLAB, WIDTH), axis=0).astype(BF16)
-
     pending.append((nearby, send_sems.at[7]))
     pending.append((distant, send_sems.at[8]))
     for store in stores:
@@ -210,26 +209,32 @@
         drain(*copy)
 
 
-def write_out(gi, gwi, gwo, gi_hbm, gwi_hbm, gwo_hbm, gi_vmem, gwi_vmem, gwo_vmem, in_sems, out_sems):
+def write_out(slabs, gwi, gwo, gi_hbm, gwi_hbm, gwo_hbm, held, gi_vmem, gwi_vmem, gwo_vmem, in_sems, out_sems):
     loads, stores = [], []
 
-    def through(source, held, target, pieces):
-        rows = source.shape[0] // pieces
-        for piece in range(pieces):
+    def through(source, buffer, target):
+        rows = source.shape[0] // PIECES
+        for piece in range(PIECES):
             part, at = pl.ds(piece * rows, rows), len(loads)
-            loads.append(pltpu.make_async_copy(source.at[part], held.at[part], in_sems.at[at]))
-            stores.append(pltpu.make_async_copy(held.at[part], target.at[part], out_sems.at[at]))
-
-    through(gwi, gwi_vmem, gwi_hbm, PIECES)
-    through(gwo, gwo_vmem, gwo_hbm, PIECES)
-    through(gi, gi_vmem, gi_hbm, 1)
+            loads.append(pltpu.make_async_copy(source.at[part], buffer.at[part], in_sems.at[at]))
+            stores.append(pltpu.make_async_copy(buffer.at[part], target.at[part], out_sems.at[at]))
+
+    through(gwi, gwi_vmem, gwi_hbm)
+    through(gwo, gwo_vmem, gwo_hbm)
+    fetch = pltpu.make_async_copy(slabs, held, in_sems.at[2 * PIECES])
+    fetch.start()
     for load in loads:
         load.start()
+    fetch.wait()
+    gi_vmem[...] = jnp.sum(held[...].astype(F32).reshape(32, SLAB, WIDTH), axis=0).astype(BF16)
+    last = pltpu.make_async_copy(gi_vmem, gi_hbm, out_sems.at[2 * PIECES])
+    last.start()
     for load, store in zip(loads, stores):
         load.wait()
         store.start()
     for store in stores:
         store.wait()
+    last.wait()
 
 
 def local(inputs, w_in, w_out, grad_out):
@@ -238,12 +243,12 @@
     outs = pl.pallas_call(
         kernel,
         out_shape=(
-            jax.ShapeDtypeStruct((SLAB, WIDTH), BF16),
+            jax.ShapeDtypeStruct((2, GROUPS, SLAB, WIDTH), BF16),
             jax.ShapeDtypeStruct((WIDTH, HIDDEN), BF16),
             jax.ShapeDtypeStruct((HIDDEN, WIDTH), BF16),
         ),
         in_specs=[hbm] * 4,
-        out_specs=(vmem, hbm, hbm),
+        out_specs=(hbm, hbm, hbm),
         scratch_shapes=[
             pltpu.VMEM((WIDTH, HIDDEN), BF16),
             pltpu.VMEM((HIDDEN, WIDTH), BF16),
@@ -256,8 +261,7 @@
             pltpu.VMEM((2, ROWS, 8, HALF), BF16),
             pltpu.VMEM((2, ROWS, 8, HALF), BF16),
             pltpu.VMEM((2, GROUPS, SLAB, WIDTH), BF16),
-            pltpu.VMEM((2, GROUPS, SLAB, WIDTH), BF16),
-            pltpu.SemaphoreType.DMA((6,)),
+            pltpu.SemaphoreType.DMA((7,)),
             pltpu.SemaphoreType.DMA((12,)),
             pltpu.SemaphoreType.DMA((12,)),
             pltpu.SemaphoreType.REGULAR,
@@ -269,11 +273,18 @@
     )(inputs, w_in, w_out, grad_out)
     return pl.pallas_call(
         write_out,
-        out_shape=tuple(jax.ShapeDtypeStruct(out.shape, out.dtype) for out in outs),
+        out_shape=(
+            jax.ShapeDtypeStruct((SLAB, WIDTH), BF16),
+            jax.ShapeDtypeStruct((WIDTH, HIDDEN), BF16),
+            jax.ShapeDtypeStruct((HIDDEN, WIDTH), BF16),
+        ),
         in_specs=[hbm, hbm, hbm],
         out_specs=(hbm, hbm, hbm),
         scratch_shapes=[
-            *[pltpu.VMEM(out.shape, out.dtype) for out in outs],
+            pltpu.VMEM((2, GROUPS, SLAB, WIDTH), BF16),
+            pltpu.VMEM((SLAB, WIDTH), BF16),
+            pltpu.VMEM((WIDTH, HIDDEN), BF16),
+            pltpu.VMEM((HIDDEN, WIDTH), BF16),
             pltpu.SemaphoreType.DMA((1 + 2 * PIECES,)),
             pltpu.SemaphoreType.DMA((1 + 2 * PIECES,)),
         ],

time: 62.9 us -> 62.5 us (level)
  no operation moved by 1% of the time
where the time goes in v3:
time: 62.5 us; the launch traced here: 62.4 us
  Pallas kernels  61.7 us (99%)
  between operations  0.64 us (1%)
    pallas_call x1, Pallas kernels, local(): pl.pallas_call(kernel, out_shape=(jax.ShapeDtypeStruct((2, GROUPS, SLAB,...  59.5 us
    pallas_call x1, Pallas kernels, local(): pl.pallas_call(write_out, out_shape=(jax.ShapeDtypeStruct((SLAB, WIDTH),...  2.19 us

profile of v3, /device:TPU:15, one launch (start us, length us, event | category | flops | bytes accessed | tf_op | source)
XLA Modules:
  0.0 62.4 jit_solution(11097864455335155639)
XLA Ops:
  0.6 59.5 %ffn_backward.1 = (bf16[2,16,4,384]{3,2,1,0:T(4,128)(2,1)}, bf16[384,768]{1,0:T(8,128)(2,1)}, bf16[768,384]{1,0:T(8,128)(2,1)}) custom-call(bf16[4,384]{1,0:T(4,128)(2,1)} %x_hbm.1, bf16[384,768]{1,0:T(8,128)(2,1)} %w_in_hbm.1, bf16[768,384]{1,0:T(8,128)(2,1)} %w_out_hbm.1, bf16[4,384]{1,0:T(4,128)(2,1)} %dy_hbm.1), custom_call_target="tpu_custom_call" | custom-call | tf_op jit(solution)/shard_map/ffn_backward/pallas_call | solution.py:243
  60.2 2.2 %write_out.1 = (bf16[4,384]{1,0:T(4,128)(2,1)}, bf16[384,768]{1,0:T(8,128)(2,1)}, bf16[768,384]{1,0:T(8,128)(2,1)}) custom-call(bf16[2,16,4,384]{3,2,1,0:T(4,128)(2,1)} %get-tuple-element.6.slabs, bf16[384,768]{1,0:T(8,128)(2,1)} %get-tuple-element.7.gwi, bf16[768,384]{1,0:T(8,128)(2,1)} %get-tuple-element.8.gwo), custom_call_target="tpu_custom_call" | custom-call | tf_op jit(solution)/shard_map/write_out/pallas_call | solution.py:274
